TPU v7x, 32 devices: a whole 2x2x4 slice. The times are simulated.
32 devices in a mesh: height: 8 (over y, x, core), plan: 4 (over z).
Axes of the slice: x: 2, y: 2, z: 4, core: 2. Of those that a mesh axis runs over, the one named last changes fastest.
Arguments:
- divergence: float32 [32, 64, 512], P('height', 'plan'), may hold values from -8 to 8
- density: float32 [32, 64, 512], P('height', 'plan'), may hold values from 0.5 to 2
- zones: int32 [32, 64, 512], P('height', 'plan'), may hold values from 0 to 4
Outputs:
- pressure: float32 [32, 64, 512], P('height', 'plan')
Inputs may be any that keep to these rules, and one draw needn't show every extreme that they name: `zones`: zone 0 open air, 1 wall, 2 stairwell, 3 open door, 4 closed door.
All inputs are finite; a program needn't handle non-finite values.
Results may differ from a plain program's by a relative error of at most 0.00002.
Values sent between devices are 32-bit elements; how exact they have to be, the bound alone decides.
A program may use at most 64 MiB of HBM per device.

v0:
```python
import jax
import jax.numpy as jnp
from jax import lax
from jax.sharding import PartitionSpec as P

PRE = 2
POST = 2
COARSE = 4


PERMEABILITY = (1.0, 0.1, 0.6, 0.8, 0.25)
OMEGA = 2.0 / 3.0


def padded_2(cells, sides, width):
    for axis, dim in sides:
        count = lax.axis_size(axis)
        ends = count - 1
        head = lax.slice_in_dim(cells, 0, width, axis=dim)
        tail = lax.slice_in_dim(cells, cells.shape[dim] - width, cells.shape[dim], axis=dim)
        cells = jnp.concatenate(
            [
                lax.ppermute(tail, axis, [(i, (i + 1) % count) for i in range(ends)]),
                cells,
                lax.ppermute(head, axis, [((i + 1) % count, i) for i in range(ends)]),
            ],
            axis=dim,
        )
    return cells


def conduct(zones, density):
    perm = jnp.zeros(density.shape, jnp.float32)
    for zone_id, value in enumerate(PERMEABILITY):
        perm = perm + jnp.where(zones == zone_id, jnp.float32(value), jnp.float32(0.0))
    return perm / density


def harmonic(first, second):
    return 2.0 * first * second / (first + second)


def neighbours(padded):
    return [
        padded[:-2, 1:-1, 1:-1],
        padded[2:, 1:-1, 1:-1],
        padded[1:-1, :-2, 1:-1],
        padded[1:-1, 2:, 1:-1],
        padded[1:-1, 1:-1, :-2],
        padded[1:-1, 1:-1, 2:],
    ]


def setup(cond, padder):
    padded = padder(cond - 1.0) + 1.0
    coeffs = [harmonic(cond, other) for other in neighbours(padded)]
    diag = coeffs[0] + coeffs[1] + coeffs[2] + coeffs[3] + coeffs[4] + coeffs[5]
    return (coeffs, diag)


def stencil(field, coeffs, padder):
    others = neighbours(padder(field))
    total = coeffs[0] * (field - others[0])
    for index in range(1, 6):
        total = total + coeffs[index] * (field - others[index])
    return total


def smooth(field, source, coeffs, diag, padder, count):
    for sweep in range(count):
        field = field + OMEGA * (source - stencil(field, coeffs, padder)) / diag
    return field


def block_sum(field):
    depth, across, along = field.shape
    return field.reshape(depth // 2, 2, across // 2, 2, along // 2, 2).sum(axis=(1, 3, 5))


def prolong(field):
    depth, across, along = field.shape
    wide = jnp.broadcast_to(field[:, None, :, None, :, None], (depth, 2, across, 2, along, 2))
    return wide.reshape(depth * 2, across * 2, along * 2)


def pad_spread(field):
    framed = padded_2(field, (("height", 0), ("plan", 1)), 1)
    return jnp.pad(framed, ((0, 0), (0, 0), (1, 1)))


def pad_column(field):
    framed = padded_2(field, (("height", 0),), 1)
    return jnp.pad(framed, ((0, 0), (1, 1), (1, 1)))


def agglomerate(source, cond):
    return (
        lax.all_gather(source, "plan", axis=1, tiled=True),
        lax.all_gather(cond, "plan", axis=1, tiled=True),
    )


def own_tile(field, width):
    return lax.dynamic_slice_in_dim(field, lax.axis_index("plan") * width, width, 1)


def coarsest(f2, cond2):
    coeffs2, diag2 = setup(cond2, pad_column)
    p2 = OMEGA * f2 / diag2
    p2 = smooth(p2, f2, coeffs2, diag2, pad_column, COARSE - 1)
    leftover = f2 - stencil(p2, coeffs2, pad_column)
    line = jnp.sum(leftover, axis=1, keepdims=True) / jnp.sum(diag2, axis=1, keepdims=True)
    return p2 + line


def on_device(divergence, density, zones):
    cond0 = conduct(zones, density)
    coeffs0, diag0 = setup(cond0, pad_spread)
    p0 = OMEGA * divergence / diag0
    p0 = smooth(p0, divergence, coeffs0, diag0, pad_spread, PRE - 1)
    f1 = 0.5 * block_sum(divergence - stencil(p0, coeffs0, pad_spread))
    cond1 = 0.125 * block_sum(cond0)
    coeffs1, diag1 = setup(cond1, pad_spread)
    p1 = OMEGA * f1 / diag1
    p1 = smooth(p1, f1, coeffs1, diag1, pad_spread, PRE - 1)
    f2 = 0.5 * block_sum(f1 - stencil(p1, coeffs1, pad_spread))
    cond2 = 0.125 * block_sum(cond1)
    width2 = f2.shape[1]
    f2, cond2 = agglomerate(f2, cond2)
    p2 = own_tile(coarsest(f2, cond2), width2)
    p1 = smooth(p1 + prolong(p2), f1, coeffs1, diag1, pad_spread, POST)
    return smooth(p0 + prolong(p1), divergence, coeffs0, diag0, pad_spread, POST)


def solution(mesh):
    return jax.shard_map(
        on_device,
        mesh=mesh,
        in_specs=(P("height", "plan", None), P("height", "plan", None), P("height", "plan", None)),
        out_specs=P("height", "plan", None),
        check_vma=False,
    )
```

profile of v0, /device:TPU:0, one launch (start us, length us, event | category | flops | bytes accessed | tf_op | source)
XLA Modules:
  0.0 251.5 jit_solution(3862618343382296736)
XLA Ops:
  13.5 9.8 %reshape.57 = f32[2,2,8,2,256,2]{5,4,3,2,1,0:T(8,128)} reshape(f32[4,16,512]{2,1,0:T(8,128)S(1)} %get-tuple-element.29) | data formatting | bytes 262144 | tf_op jit(solution)/shard_map/reshape | solution.py:77
  23.3 4.0 %reduce_sum.69 = f32[2,8,256]{2,1,0:T(8,128)S(1)} reduce(f32[2,2,8,2,256,2]{5,4,3,2,1,0:T(8,128)} %reshape.57, f32[]{:T(128)} %constant.22.clone.1), dimensions={1,3,5}, to_apply=%region_1.2 | reduce | flops 28672 | bytes 147460 | tf_op jit(solution)/shard_map/reduce_sum | solution.py:77
  27.8 4.3 %collective-permute-start.4 = (f32[1,16,512]{2,1,0:T(8,128)S(1)}, f32[1,16,512]{2,1,0:T(8,128)S(1)}, u32[]{:S(2)}, u32[]{:S(2)}) collective-permute-start(f32[1,16,512]{2,1,0:T(8,128)S(1)} %get-tuple-element.46), channel_id=1, source_target_pairs={{0,4},{4,8},{8,12},{12,16},{16,20},{20,24},{24,28},{1,5},{5,9},{9,... | collective-permute-start | bytes 98312 | tf_op jit(solution)/shard_map/ppermute | solution.py:23
  35.2 4.3 %collective-permute-start.6 = (f32[6,1,512]{2,1,0:T(1,128)S(1)}, f32[6,1,512]{2,1,0:T(1,128)S(1)}, u32[]{:S(2)}, u32[]{:S(2)}) collective-permute-start(f32[6,1,512]{2,1,0:T(1,128)S(1)} %get-tuple-element.36), channel_id=1, source_target_pairs={{0,1},{1,2},{2,3},{4,5},{5,6},{6,7},{8,9},{9,10},{10,11},{12,13},{... | collective-permute-start | bytes 36872 | tf_op jit(solution)/shard_map/ppermute | solution.py:23
  40.9 4.5 %collective-permute-start.12 = (f32[1,8,256]{2,1,0:T(8,128)S(1)}, f32[1,8,256]{2,1,0:T(8,128)S(1)}, u32[]{:S(2)}, u32[]{:S(2)}) collective-permute-start(f32[1,8,256]{2,1,0:T(8,128)S(1)} %get-tuple-element.69), channel_id=1, source_target_pairs={{0,4},{4,8},{8,12},{12,16},{16,20},{20,24},{24,28},{1,5},{5,9},{9,... | collective-permute-start | bytes 24584 | tf_op jit(solution)/shard_map/ppermute | solution.py:23
  51.5 4.3 %collective-permute-start.14 = (f32[4,1,256]{2,1,0:T(1,128)S(1)}, f32[4,1,256]{2,1,0:T(1,128)S(1)}, u32[]{:S(2)}, u32[]{:S(2)}) collective-permute-start(f32[4,1,256]{2,1,0:T(1,128)S(1)} %get-tuple-element.58), channel_id=1, source_target_pairs={{0,1},{1,2},{2,3},{4,5},{5,6},{6,7},{8,9},{9,10},{10,11},{12,13},{... | collective-permute-start | bytes 12296 | tf_op jit(solution)/shard_map/ppermute | solution.py:23
  57.2 4.5 %collective-permute-start.10 = (f32[6,1,512]{2,1,0:T(1,128)S(1)}, f32[6,1,512]{2,1,0:T(1,128)S(1)}, u32[]{:S(2)}, u32[]{:S(2)}) collective-permute-start(f32[6,1,512]{2,1,0:T(1,128)S(1)} %get-tuple-element.34), channel_id=1, source_target_pairs={{0,1},{1,2},{2,3},{4,5},{5,6},{6,7},{8,9},{9,10},{10,11},{12,13},{... | collective-permute-start | bytes 36872 | tf_op jit(solution)/shard_map/ppermute | solution.py:23
  63.2 4.1 %collective-permute-done.11 = f32[6,1,512]{2,1,0:T(1,128)S(1)} collective-permute-done((f32[6,1,512]{2,1,0:T(1,128)S(1)}, f32[6,1,512]{2,1,0:T(1,128)S(1)}, u32[]{:S(2)}, u32[]{:S(2)}) %collective-permute-start.11) | collective-permute-done | bytes 12320 | tf_op jit(solution)/shard_map/ppermute | solution.py:25
  67.7 9.8 %reshape.56 = f32[2,2,8,2,256,2]{5,4,3,2,1,0:T(8,128)} reshape(f32[4,16,512]{2,1,0:T(8,128)S(1)} %fusion.42) | data formatting | bytes 262144 | tf_op jit(solution)/shard_map/reshape | solution.py:77
  77.5 4.0 %reduce_sum.68 = f32[2,8,256]{2,1,0:T(8,128)S(1)} reduce(f32[2,2,8,2,256,2]{5,4,3,2,1,0:T(8,128)} %reshape.56, f32[]{:T(128)} %constant.22.clone.1), dimensions={1,3,5}, to_apply=%region_0.1 | reduce | flops 28672 | bytes 147460 | tf_op jit(solution)/shard_map/reduce_sum | solution.py:77
  86.8 4.4 %collective-permute-done.17 = f32[1,8,256]{2,1,0:T(8,128)S(1)} collective-permute-done((f32[1,8,256]{2,1,0:T(8,128)S(1)}, f32[1,8,256]{2,1,0:T(8,128)S(1)}, u32[]{:S(2)}, u32[]{:S(2)}) %collective-permute-start.17) | collective-permute-done | bytes 8224 | tf_op jit(solution)/shard_map/ppermute | solution.py:25
  96.0 13.2 %all-gather.3 = f32[4,4,128]{2,1,0:T(4,128)S(1)} all-gather(f32[1,4,128]{2,1,0:T(4,128)S(1)} %multiply_bitcast_fusion), channel_id=3, replica_groups=mesh['height'=8,'plan'=4] {'plan'}, dimensions={0}, use_global_device_ids=true | all-gather | bytes 10240 | tf_op jit(solution)/shard_map/all_gather | solution.py:99
  112.0 7.2 %collective-permute-start.24 = (f32[1,16,128]{2,1,0:T(8,128)S(1)}, f32[1,16,128]{2,1,0:T(8,128)S(1)}, u32[]{:S(2)}, u32[]{:S(2)}) collective-permute-start(f32[1,16,128]{2,1,0:T(8,128)S(1)} %bitcast_add_fusion.6), channel_id=1, source_target_pairs={{0,4},{4,8},{8,12},{12,16},{16,20},{20,24},{24,28},{1,5},{5,9},{9,... | collective-permute-start | bytes 24584 | tf_op jit(solution)/shard_map/ppermute | solution.py:23
  123.9 4.1 %collective-permute-done.23 = f32[4,1,256]{2,1,0:T(1,128)S(1)} collective-permute-done((f32[4,1,256]{2,1,0:T(1,128)S(1)}, f32[4,1,256]{2,1,0:T(1,128)S(1)}, u32[]{:S(2)}, u32[]{:S(2)}) %collective-permute-start.23) | collective-permute-done | bytes 4128 | tf_op jit(solution)/shard_map/ppermute | solution.py:25
  128.8 11.9 %all-gather.2 = f32[4,4,128]{2,1,0:T(4,128)S(1)} all-gather(f32[1,4,128]{2,1,0:T(4,128)S(1)} %multiply_bitcast_fusion.1), channel_id=2, replica_groups=mesh['height'=8,'plan'=4] {'plan'}, dimensions={0}, use_global_device_ids=true | all-gather | bytes 10240 | tf_op jit(solution)/shard_map/all_gather | solution.py:98
  143.4 6.0 %collective-permute-done.27 = f32[1,16,128]{2,1,0:T(8,128)S(1)} collective-permute-done((f32[1,16,128]{2,1,0:T(8,128)S(1)}, f32[1,16,128]{2,1,0:T(8,128)S(1)}, u32[]{:S(2)}, u32[]{:S(2)}) %collective-permute-start.27) | collective-permute-done | bytes 8224 | tf_op jit(solution)/shard_map/ppermute | solution.py:25
  149.5 4.3 %collective-permute-start.28 = (f32[1,16,128]{2,1,0:T(8,128)S(1)}, f32[1,16,128]{2,1,0:T(8,128)S(1)}, u32[]{:S(2)}, u32[]{:S(2)}) collective-permute-start(f32[1,16,128]{2,1,0:T(8,128)S(1)} %fusion.196), channel_id=1, source_target_pairs={{0,4},{4,8},{8,12},{12,16},{16,20},{20,24},{24,28},{1,5},{5,9},{9,... | collective-permute-start | bytes 24584 | tf_op jit(solution)/shard_map/ppermute | solution.py:23
  159.3 5.9 %collective-permute-start.30 = (f32[1,16,128]{2,1,0:T(8,128)S(1)}, f32[1,16,128]{2,1,0:T(8,128)S(1)}, u32[]{:S(2)}, u32[]{:S(2)}) collective-permute-start(f32[1,16,128]{2,1,0:T(8,128)S(1)} %fusion.184), channel_id=1, source_target_pairs={{0,4},{4,8},{8,12},{12,16},{16,20},{20,24},{24,28},{1,5},{5,9},{9,... | collective-permute-start | bytes 24584 | tf_op jit(solution)/shard_map/ppermute | solution.py:23
  168.5 4.7 %collective-permute-start.32 = (f32[1,16,128]{2,1,0:T(8,128)S(1)}, f32[1,16,128]{2,1,0:T(8,128)S(1)}, u32[]{:S(2)}, u32[]{:S(2)}) collective-permute-start(f32[1,16,128]{2,1,0:T(8,128)S(1)} %fusion.172), channel_id=1, source_target_pairs={{0,4},{4,8},{8,12},{12,16},{16,20},{20,24},{24,28},{1,5},{5,9},{9,... | collective-permute-start | bytes 24584 | tf_op jit(solution)/shard_map/ppermute | solution.py:23
  176.9 4.7 %collective-permute-start.34 = (f32[1,8,256]{2,1,0:T(8,128)S(1)}, f32[1,8,256]{2,1,0:T(8,128)S(1)}, u32[]{:S(2)}, u32[]{:S(2)}) collective-permute-start(f32[1,8,256]{2,1,0:T(8,128)S(1)} %get-tuple-element.62), channel_id=1, source_target_pairs={{0,4},{4,8},{8,12},{12,16},{16,20},{20,24},{24,28},{1,5},{5,9},{9,... | collective-permute-start | bytes 24584 | tf_op jit(solution)/shard_map/ppermute | solution.py:23
  188.0 4.2 %collective-permute-done.37 = f32[4,1,256]{2,1,0:T(1,128)S(1)} collective-permute-done((f32[4,1,256]{2,1,0:T(1,128)S(1)}, f32[4,1,256]{2,1,0:T(1,128)S(1)}, u32[]{:S(2)}, u32[]{:S(2)}) %collective-permute-start.37) | collective-permute-done | bytes 4128 | tf_op jit(solution)/shard_map/ppermute | solution.py:25
  212.7 6.9 %reshape.58 = f32[4,16,512]{2,1,0:T(8,128)S(1)} reshape(f32[2,2,8,2,256,2]{5,4,3,2,1,0:T(8,128)} %broadcast_in_dim.54) | data formatting | bytes 262144 | tf_op jit(solution)/shard_map/reshape | solution.py:83
  230.4 4.2 %collective-permute-done.45 = f32[6,1,512]{2,1,0:T(1,128)S(1)} collective-permute-done((f32[6,1,512]{2,1,0:T(1,128)S(1)}, f32[6,1,512]{2,1,0:T(1,128)S(1)}, u32[]{:S(2)}, u32[]{:S(2)}) %collective-permute-start.45) | collective-permute-done | bytes 12320 | tf_op jit(solution)/shard_map/ppermute | solution.py:25
  246.3 4.2 %collective-permute-done.49 = f32[6,1,512]{2,1,0:T(1,128)S(1)} collective-permute-done((f32[6,1,512]{2,1,0:T(1,128)S(1)}, f32[6,1,512]{2,1,0:T(1,128)S(1)}, u32[]{:S(2)}, u32[]{:S(2)}) %collective-permute-start.49) | collective-permute-done | bytes 12320 | tf_op jit(solution)/shard_map/ppermute | solution.py:25
  (151 shorter events, 111.0 us)
Async XLA Ops:
  8.7 18.6 %collective-permute-start.2 = (f32[6,1,512]{2,1,0:T(1,128)S(1)}, f32[6,1,512]{2,1,0:T(1,128)S(1)}, u32[]{:S(2)}, u32[]{:S(2)}) collective-permute-start(f32[6,1,512]{2,1,0:T(1,128)S(1)} %get-tuple-element.38), channel_id=1, source_target_pairs={{0,1},{1,2},{2,3},{4,5},{5,6},{6,7},{8,9},{9,10},{10,11},{12,13},{... | collective-permute-start | bytes 36872 | tf_op jit(solution)/shard_map/ppermute | solution.py:23
  12.1 15.1 %collective-permute-start.3 = (f32[6,1,512]{2,1,0:T(1,128)S(1)}, f32[6,1,512]{2,1,0:T(1,128)S(1)}, u32[]{:S(2)}, u32[]{:S(2)}) collective-permute-start(f32[6,1,512]{2,1,0:T(1,128)S(1)} %get-tuple-element.39), channel_id=1, source_target_pairs={{1,0},{2,1},{3,2},{5,4},{6,5},{7,6},{9,8},{10,9},{11,10},{13,12},{... | collective-permute-start | bytes 36872 | tf_op jit(solution)/shard_map/ppermute | solution.py:25
  35.2 11.4 %collective-permute-start.6 = (f32[6,1,512]{2,1,0:T(1,128)S(1)}, f32[6,1,512]{2,1,0:T(1,128)S(1)}, u32[]{:S(2)}, u32[]{:S(2)}) collective-permute-start(f32[6,1,512]{2,1,0:T(1,128)S(1)} %get-tuple-element.36), channel_id=1, source_target_pairs={{0,1},{1,2},{2,3},{4,5},{5,6},{6,7},{8,9},{9,10},{10,11},{12,13},{... | collective-permute-start | bytes 36872 | tf_op jit(solution)/shard_map/ppermute | solution.py:23
  39.6 7.1 %collective-permute-start.7 = (f32[6,1,512]{2,1,0:T(1,128)S(1)}, f32[6,1,512]{2,1,0:T(1,128)S(1)}, u32[]{:S(2)}, u32[]{:S(2)}) collective-permute-start(f32[6,1,512]{2,1,0:T(1,128)S(1)} %get-tuple-element.37), channel_id=1, source_target_pairs={{1,0},{2,1},{3,2},{5,4},{6,5},{7,6},{9,8},{10,9},{11,10},{13,12},{... | collective-permute-start | bytes 36872 | tf_op jit(solution)/shard_map/ppermute | solution.py:25
  40.9 10.6 %collective-permute-start.12 = (f32[1,8,256]{2,1,0:T(8,128)S(1)}, f32[1,8,256]{2,1,0:T(8,128)S(1)}, u32[]{:S(2)}, u32[]{:S(2)}) collective-permute-start(f32[1,8,256]{2,1,0:T(8,128)S(1)} %get-tuple-element.69), channel_id=1, source_target_pairs={{0,4},{4,8},{8,12},{12,16},{16,20},{20,24},{24,28},{1,5},{5,9},{9,... | collective-permute-start | bytes 24584 | tf_op jit(solution)/shard_map/ppermute | solution.py:23
  45.4 6.1 %collective-permute-start.13 = (f32[1,8,256]{2,1,0:T(8,128)S(1)}, f32[1,8,256]{2,1,0:T(8,128)S(1)}, u32[]{:S(2)}, u32[]{:S(2)}) collective-permute-start(f32[1,8,256]{2,1,0:T(8,128)S(1)} %get-tuple-element.70), channel_id=1, source_target_pairs={{4,0},{8,4},{12,8},{16,12},{20,16},{24,20},{28,24},{5,1},{9,5},{13... | collective-permute-start | bytes 24584 | tf_op jit(solution)/shard_map/ppermute | solution.py:25
  47.1 10.0 %collective-permute-start.8 = (f32[1,16,512]{2,1,0:T(8,128)S(1)}, f32[1,16,512]{2,1,0:T(8,128)S(1)}, u32[]{:S(2)}, u32[]{:S(2)}) collective-permute-start(f32[1,16,512]{2,1,0:T(8,128)S(1)} %get-tuple-element.44), channel_id=1, source_target_pairs={{0,4},{4,8},{8,12},{12,16},{16,20},{20,24},{24,28},{1,5},{5,9},{9,... | collective-permute-start | bytes 98312 | tf_op jit(solution)/shard_map/ppermute | solution.py:23
  50.2 7.0 %collective-permute-start.9 = (f32[1,16,512]{2,1,0:T(8,128)S(1)}, f32[1,16,512]{2,1,0:T(8,128)S(1)}, u32[]{:S(2)}, u32[]{:S(2)}) collective-permute-start(f32[1,16,512]{2,1,0:T(8,128)S(1)} %get-tuple-element.45), channel_id=1, source_target_pairs={{4,0},{8,4},{12,8},{16,12},{20,16},{24,20},{28,24},{5,1},{9,5},{13... | collective-permute-start | bytes 98312 | tf_op jit(solution)/shard_map/ppermute | solution.py:25
  51.5 11.6 %collective-permute-start.14 = (f32[4,1,256]{2,1,0:T(1,128)S(1)}, f32[4,1,256]{2,1,0:T(1,128)S(1)}, u32[]{:S(2)}, u32[]{:S(2)}) collective-permute-start(f32[4,1,256]{2,1,0:T(1,128)S(1)} %get-tuple-element.58), channel_id=1, source_target_pairs={{0,1},{1,2},{2,3},{4,5},{5,6},{6,7},{8,9},{9,10},{10,11},{12,13},{... | collective-permute-start | bytes 12296 | tf_op jit(solution)/shard_map/ppermute | solution.py:23
  55.8 7.2 %collective-permute-start.15 = (f32[4,1,256]{2,1,0:T(1,128)S(1)}, f32[4,1,256]{2,1,0:T(1,128)S(1)}, u32[]{:S(2)}, u32[]{:S(2)}) collective-permute-start(f32[4,1,256]{2,1,0:T(1,128)S(1)} %get-tuple-element.59), channel_id=1, source_target_pairs={{1,0},{2,1},{3,2},{5,4},{6,5},{7,6},{9,8},{10,9},{11,10},{13,12},{... | collective-permute-start | bytes 12296 | tf_op jit(solution)/shard_map/ppermute | solution.py:25
  57.2 6.0 %collective-permute-start.10 = (f32[6,1,512]{2,1,0:T(1,128)S(1)}, f32[6,1,512]{2,1,0:T(1,128)S(1)}, u32[]{:S(2)}, u32[]{:S(2)}) collective-permute-start(f32[6,1,512]{2,1,0:T(1,128)S(1)} %get-tuple-element.34), channel_id=1, source_target_pairs={{0,1},{1,2},{2,3},{4,5},{5,6},{6,7},{8,9},{9,10},{10,11},{12,13},{... | collective-permute-start | bytes 36872 | tf_op jit(solution)/shard_map/ppermute | solution.py:23
  61.7 5.6 %collective-permute-start.11 = (f32[6,1,512]{2,1,0:T(1,128)S(1)}, f32[6,1,512]{2,1,0:T(1,128)S(1)}, u32[]{:S(2)}, u32[]{:S(2)}) collective-permute-start(f32[6,1,512]{2,1,0:T(1,128)S(1)} %get-tuple-element.35), channel_id=1, source_target_pairs={{1,0},{2,1},{3,2},{5,4},{6,5},{7,6},{9,8},{10,9},{11,10},{13,12},{... | collective-permute-start | bytes 36872 | tf_op jit(solution)/shard_map/ppermute | solution.py:25
  84.8 6.3 %collective-permute-start.17 = (f32[1,8,256]{2,1,0:T(8,128)S(1)}, f32[1,8,256]{2,1,0:T(8,128)S(1)}, u32[]{:S(2)}, u32[]{:S(2)}) collective-permute-start(f32[1,8,256]{2,1,0:T(8,128)S(1)} %get-tuple-element.68), channel_id=1, source_target_pairs={{4,0},{8,4},{12,8},{16,12},{20,16},{24,20},{28,24},{5,1},{9,5},{13... | collective-permute-start | bytes 24584 | tf_op jit(solution)/shard_map/ppermute | solution.py:25
  91.1 18.0 %collective-permute-start.18 = (f32[4,1,256]{2,1,0:T(1,128)S(1)}, f32[4,1,256]{2,1,0:T(1,128)S(1)}, u32[]{:S(2)}, u32[]{:S(2)}) collective-permute-start(f32[4,1,256]{2,1,0:T(1,128)S(1)} %get-tuple-element.56), channel_id=1, source_target_pairs={{0,1},{1,2},{2,3},{4,5},{5,6},{6,7},{8,9},{9,10},{10,11},{12,13},{... | collective-permute-start | bytes 12296 | tf_op jit(solution)/shard_map/ppermute | solution.py:23
  94.6 14.5 %collective-permute-start.19 = (f32[4,1,256]{2,1,0:T(1,128)S(1)}, f32[4,1,256]{2,1,0:T(1,128)S(1)}, u32[]{:S(2)}, u32[]{:S(2)}) collective-permute-start(f32[4,1,256]{2,1,0:T(1,128)S(1)} %get-tuple-element.57), channel_id=1, source_target_pairs={{1,0},{2,1},{3,2},{5,4},{6,5},{7,6},{9,8},{10,9},{11,10},{13,12},{... | collective-permute-start | bytes 12296 | tf_op jit(solution)/shard_map/ppermute | solution.py:25
  109.4 11.1 %collective-permute-start.20 = (f32[1,8,256]{2,1,0:T(8,128)S(1)}, f32[1,8,256]{2,1,0:T(8,128)S(1)}, u32[]{:S(2)}, u32[]{:S(2)}) collective-permute-start(f32[1,8,256]{2,1,0:T(8,128)S(1)} %get-tuple-element.65), channel_id=1, source_target_pairs={{0,4},{4,8},{8,12},{12,16},{16,20},{20,24},{24,28},{1,5},{5,9},{9,... | collective-permute-start | bytes 24584 | tf_op jit(solution)/shard_map/ppermute | solution.py:23
  110.7 9.9 %collective-permute-start.21 = (f32[1,8,256]{2,1,0:T(8,128)S(1)}, f32[1,8,256]{2,1,0:T(8,128)S(1)}, u32[]{:S(2)}, u32[]{:S(2)}) collective-permute-start(f32[1,8,256]{2,1,0:T(8,128)S(1)} %get-tuple-element.66), channel_id=1, source_target_pairs={{4,0},{8,4},{12,8},{16,12},{20,16},{24,20},{28,24},{5,1},{9,5},{13... | collective-permute-start | bytes 24584 | tf_op jit(solution)/shard_map/ppermute | solution.py:25
  112.0 11.8 %collective-permute-start.24 = (f32[1,16,128]{2,1,0:T(8,128)S(1)}, f32[1,16,128]{2,1,0:T(8,128)S(1)}, u32[]{:S(2)}, u32[]{:S(2)}) collective-permute-start(f32[1,16,128]{2,1,0:T(8,128)S(1)} %bitcast_add_fusion.6), channel_id=1, source_target_pairs={{0,4},{4,8},{8,12},{12,16},{16,20},{20,24},{24,28},{1,5},{5,9},{9,... | collective-permute-start | bytes 24584 | tf_op jit(solution)/shard_map/ppermute | solution.py:23
  142.1 7.3 %collective-permute-start.27 = (f32[1,16,128]{2,1,0:T(8,128)S(1)}, f32[1,16,128]{2,1,0:T(8,128)S(1)}, u32[]{:S(2)}, u32[]{:S(2)}) collective-permute-start(f32[1,16,128]{2,1,0:T(8,128)S(1)} %get-tuple-element.7), channel_id=1, source_target_pairs={{4,0},{8,4},{12,8},{16,12},{20,16},{24,20},{28,24},{5,1},{9,5},{13... | collective-permute-start | bytes 24584 | tf_op jit(solution)/shard_map/ppermute | solution.py:25
  149.5 5.6 %collective-permute-start.28 = (f32[1,16,128]{2,1,0:T(8,128)S(1)}, f32[1,16,128]{2,1,0:T(8,128)S(1)}, u32[]{:S(2)}, u32[]{:S(2)}) collective-permute-start(f32[1,16,128]{2,1,0:T(8,128)S(1)} %fusion.196), channel_id=1, source_target_pairs={{0,4},{4,8},{8,12},{12,16},{16,20},{20,24},{24,28},{1,5},{5,9},{9,... | collective-permute-start | bytes 24584 | tf_op jit(solution)/shard_map/ppermute | solution.py:23
  159.3 7.2 %collective-permute-start.30 = (f32[1,16,128]{2,1,0:T(8,128)S(1)}, f32[1,16,128]{2,1,0:T(8,128)S(1)}, u32[]{:S(2)}, u32[]{:S(2)}) collective-permute-start(f32[1,16,128]{2,1,0:T(8,128)S(1)} %fusion.184), channel_id=1, source_target_pairs={{0,4},{4,8},{8,12},{12,16},{16,20},{20,24},{24,28},{1,5},{5,9},{9,... | collective-permute-start | bytes 24584 | tf_op jit(solution)/shard_map/ppermute | solution.py:23
  168.5 6.1 %collective-permute-start.32 = (f32[1,16,128]{2,1,0:T(8,128)S(1)}, f32[1,16,128]{2,1,0:T(8,128)S(1)}, u32[]{:S(2)}, u32[]{:S(2)}) collective-permute-start(f32[1,16,128]{2,1,0:T(8,128)S(1)} %fusion.172), channel_id=1, source_target_pairs={{0,4},{4,8},{8,12},{12,16},{16,20},{20,24},{24,28},{1,5},{5,9},{9,... | collective-permute-start | bytes 24584 | tf_op jit(solution)/shard_map/ppermute | solution.py:23
  176.9 6.1 %collective-permute-start.34 = (f32[1,8,256]{2,1,0:T(8,128)S(1)}, f32[1,8,256]{2,1,0:T(8,128)S(1)}, u32[]{:S(2)}, u32[]{:S(2)}) collective-permute-start(f32[1,8,256]{2,1,0:T(8,128)S(1)} %get-tuple-element.62), channel_id=1, source_target_pairs={{0,4},{4,8},{8,12},{12,16},{16,20},{20,24},{24,28},{1,5},{5,9},{9,... | collective-permute-start | bytes 24584 | tf_op jit(solution)/shard_map/ppermute | solution.py:23
  244.9 5.6 %collective-permute-start.49 = (f32[6,1,512]{2,1,0:T(1,128)S(1)}, f32[6,1,512]{2,1,0:T(1,128)S(1)}, u32[]{:S(2)}, u32[]{:S(2)}) collective-permute-start(f32[6,1,512]{2,1,0:T(1,128)S(1)} %get-tuple-element.31), channel_id=1, source_target_pairs={{1,0},{2,1},{3,2},{5,4},{6,5},{7,6},{9,8},{10,9},{11,10},{13,12},{... | collective-permute-start | bytes 36872 | tf_op jit(solution)/shard_map/ppermute | solution.py:25
  (27 other events, 125.1 us)
where the time goes:
time: 256 us; the launch traced here: 252 us
  starting transfers between devices  120 us (47%)
  waiting for transfers between devices  59.3 us (23%)
  local copies, waits for them, and re-layouts  31.8 us (12%)
  blocking collectives  25.1 us (10%)
  other arithmetic  14.3 us (6%)
    ppermute x25, starting transfers between devices, padded_2(): lax.ppermute(tail, axis, [(i, (i + 1) % count) for i in range(ends)])  87.7 us
    ppermute x25, waiting for transfers between devices, padded_2(): lax.ppermute(head, axis, [((i + 1) % count, i) for i in range(ends)])  59 us
    ppermute x25, starting transfers between devices, padded_2(): lax.ppermute(head, axis, [((i + 1) % count, i) for i in range(ends)])  32.5 us
    reshape x2, local copies, waits for them, and re-layouts, block_sum(): field.reshape(depth // 2, 2, across // 2, 2, along // 2, 2)  19.6 us
    all_gather x1, blocking collectives, agglomerate(): lax.all_gather(cond, 'plan', axis=1, tiled=True)  13.2 us
    all_gather x1, blocking collectives, agglomerate(): lax.all_gather(source, 'plan', axis=1, tiled=True)  11.9 us
    reduce_sum x5, other arithmetic, block_sum(): field.reshape(depth // 2, 2, across // 2, 2, along // 2, 2)  8.42 us
    reshape x1, local copies, waits for them, and re-layouts, prolong(): return wide.reshape(depth * 2, across * 2, along * 2)  6.94 us
  transfers between devices with their start and end apart: 50, of which 19 were waited for; matrix products, arithmetic and copies ran while one was open for 6% of the time, Pallas kernels for 0%

commit v1 on v0

v1 whole, which is shorter than its diff:
```python
import functools

import jax
import jax.numpy as jnp
from jax import lax
from jax.experimental import pallas as pl
from jax.experimental.pallas import tpu as pltpu
from jax.sharding import PartitionSpec as P

PERMEABILITY = (1.0, 0.1, 0.6, 0.8, 0.25)
OMEGA = 2.0 / 3.0
KEEP = 1.0 / 3.0
MESH = pl.DeviceIdType.MESH
F32 = jnp.float32
LANES = 128

SIDES = (1, -1)
DIAGONALS = ((1, 1), (1, -1), (-1, 1), (-1, -1))
AROUND = tuple((a, b) for a in (-1, 0, 1) for b in (-1, 0, 1) if (a, b) != (0, 0))
WIDE = tuple((a, b) for a in (-2, -1, 0, 1, 2) for b in (-1, 0, 1) if (a, b) != (0, 0))


def harmonic(a, b):
    return 2.0 * a * b / (a + b)


def lane_of(a):
    return lax.broadcasted_iota(jnp.int32, a.shape, a.ndim - 1)


def lane_prev(a, fill):
    return jnp.where(lane_of(a) == 0, fill, pltpu.roll(a, 1, a.ndim - 1))


def lane_next(a, fill):
    return jnp.where(lane_of(a) == LANES - 1, fill, pltpu.roll(a, LANES - 1, a.ndim - 1))


def y_prev(a, fill):
    return jnp.concatenate([lane_prev(a[:, -1:], fill), a[:, :-1]], axis=1)


def y_next(a, fill):
    return jnp.concatenate([a[:, 1:], lane_next(a[:, :1], fill)], axis=1)


def x_prev(a):
    return pltpu.roll(a, 1, a.ndim - 2)


def x_next(a):
    return pltpu.roll(a, a.shape[-2] - 1, a.ndim - 2)


def setup(c, inside):
    cz = harmonic(c[:-1], c[1:])
    m = c[1:-1]
    cx = harmonic(m, x_next(m))
    cxl = x_prev(cx)
    cyl = harmonic(m, y_prev(m, 1.0))
    cyu = y_next(cyl, harmonic(m[:, -1:], jnp.ones_like(m[:, -1:])))
    diag = cz[:-1] + cz[1:] + cx + cxl + cyl + cyu
    w = jnp.where(inside, OMEGA / diag, 0.0)
    return (cz, cx, cxl, cyl, cyu, diag, w)


def trim(k):
    return tuple(part[1:-1] for part in k)


def gathered(p, k):
    cz, cx, cxl, cyl, cyu = k[:5]
    m = p[1:-1]
    return (cz[:-1] * p[:-2] + cz[1:] * p[2:] + cx * x_next(m) + cxl * x_prev(m)
            + cyl * y_prev(m, 0.0) + cyu * y_next(m, 0.0))


def sweep(p, f, k):
    return KEEP * p[1:-1] + k[6] * (f + gathered(p, k))


def residual(p, f, k):
    return f - k[5] * p[1:-1] + gathered(p, k)


def paired(a):
    z, v = a.shape[:2]
    rows = []
    for i in range(0, z, 2):
        both = a[i] + a[i + 1]
        rows.append(jnp.stack([both[q] + both[q + 1] for q in range(0, v, 2)], axis=0))
    return jnp.stack(rows, axis=0)


def split3(a):
    one = a.astype(jnp.bfloat16)
    rest = a - one.astype(F32)
    two = rest.astype(jnp.bfloat16)
    three = (rest - two.astype(F32)).astype(jnp.bfloat16)
    return jnp.concatenate([one, two, three], axis=0)


def kernel(H, PL, W, layers, window, div_ref, den_ref, zon_ref, out_ref,
           CN, DN, ZC, ZD, XS, XR, GS, GR, CA, DA, C1, F1, P1, C2O, F2O, C2G, F2G,
           PN, PZ, PXS, PXR, PGS, PGR, PA, S0, S1, Q2, Q1, P2, X2C, X2F,
           ssem, rsem, gssem, grsem):
    h = lax.axis_index("height")
    j = lax.axis_index("plan")
    base = h - W if window else 0

    def exists(dh, dj):
        ok = None
        for at, step, count in ((h, dh, H), (j, dj, PL)):
            if step > 0:
                term = at + step < count
            elif step < 0:
                term = at + step >= 0
            else:
                continue
            ok = term if ok is None else jnp.logical_and(ok, term)
        return ok

    barrier = pltpu.get_barrier_semaphore()
    if window:
        for dh in range(-W, W + 1):
            @pl.when(jnp.logical_and(h + dh >= 0, h + dh < H))
            def _():
                for dj in range(PL):
                    if (dh, dj) != (0, 0):
                        pl.semaphore_signal(barrier, inc=1, device_id=(h + dh, lax.rem(j + dj, PL)), device_id_type=MESH)
    else:
        for a in range(H):
            for b in range(PL):
                if (a, b) != (0, 0):
                    pl.semaphore_signal(barrier, inc=1, device_id=(lax.rem(h + a, H), lax.rem(j + b, PL)), device_id_type=MESH)

    zones = zon_ref[...]
    perm = jnp.zeros(zones.shape, F32)
    for zone_id, value in enumerate(PERMEABILITY):
        perm = jnp.where(zones == zone_id, F32(value), perm)
    cond = perm / den_ref[...]
    ys = lax.broadcasted_iota(jnp.int32, (512, 512), 0)
    cs = lax.broadcasted_iota(jnp.int32, (512, 512), 1)
    order = (ys == 4 * (cs % LANES) + cs // LANES).astype(F32).astype(jnp.bfloat16)
    both = jnp.concatenate([cond.reshape(64, 512), div_ref[...].reshape(64, 512)], axis=0)
    moved = jnp.dot(split3(both), order, preferred_element_type=F32)
    moved = moved[0:128] + moved[128:256] + moved[256:384]
    for v in range(4):
        part = moved[:, v * LANES:(v + 1) * LANES]
        CN[:, v] = part[0:64].reshape(4, 16, LANES)
        DN[:, v] = part[64:128].reshape(4, 16, LANES)
    c = CN[...]
    d = DN[...]
    XS[0, :, :, 0:3] = c[:, :, 13:16]
    XS[0, :, :, 3:5] = d[:, :, 14:16]
    XS[1, :, :, 0:3] = c[:, :, 0:3]
    XS[1, :, :, 3:5] = d[:, :, 0:2]
    for n, (dh, dj) in enumerate(DIAGONALS):
        near, far = (3, 2) if dh > 0 else (0, 1)
        row = 15 if dj > 0 else 0
        two = 14 if dj > 0 else 0
        GS[n, :, 0:2] = c[near, :, two:two + 2]
        GS[n, :, 2:3] = c[far, :, row:row + 1]
        GS[n, :, 3:4] = d[near, :, row:row + 1]

    index = [0]

    def copies(items):
        made = []
        for dh, dj, src, dst in items:
            n = index[0]
            index[0] += 1
            copy = pltpu.make_async_remote_copy(
                src_ref=src, dst_ref=dst, send_sem=ssem.at[n], recv_sem=rsem.at[n],
                device_id=(h + dh, j + dj), device_id_type=MESH)
            made.append((exists(dh, dj), exists(-dh, -dj), copy))
        return made

    def start(made):
        for there, _, copy in made:
            pl.when(there)(copy.start)

    def arrive(made):
        for _, back, copy in made:
            pl.when(back)(copy.wait_recv)

    def sent(made):
        for there, _, copy in made:
            pl.when(there)(copy.wait_send)

    def tiles(ref, around):
        return copies([(dh, dj, ref.at[4:6, :, 8:16], ref.at[4 - 2 * dh:6 - 2 * dh, :, 8 - 8 * dj:16 - 8 * dj])
                       for dh, dj in around])

    def gather_loop(act):
        if window:
            for dh in range(-W, W + 1):
                for b in range(PL):
                    if (dh, b) != (0, 0):
                        yes = jnp.logical_and(h + dh >= 0, h + dh < H)
                        pl.when(yes)(functools.partial(act, dh, b))
        else:
            for a in range(H):
                for b in range(PL):
                    if (a, b) != (0, 0):
                        act(a, b)

    def gather_copy(which, src, buf, a, b):
        if window:
            to, mine, n = h + a, W - a, a + W
        else:
            to, mine, n = lax.rem(h + a, H), h, a
        return pltpu.make_async_remote_copy(
            src_ref=src, dst_ref=buf.at[mine, j], send_sem=gssem.at[which, n, b],
            recv_sem=grsem.at[which, n, b], device_id=(to, lax.rem(j + b, PL)), device_id_type=MESH)

    def gather_in(which, src, buf, a, b):
        gather_copy(which, src, buf, a, b).wait_recv()

    def gather_in_loop(which, src, buf):
        if window:
            for dh in range(-W, W + 1):
                for b in range(PL):
                    if (dh, b) != (0, 0):
                        yes = jnp.logical_and(h - dh >= 0, h - dh < H)
                        pl.when(yes)(functools.partial(gather_in, which, src, buf, dh, b))
        else:
            gather_loop(functools.partial(gather_in, which, src, buf))

    count = None
    if window:
        low = jnp.minimum(h, W)
        high = jnp.minimum(H - 1 - h, W)
        count = (low + high + 1) * PL - 1
    else:
        count = H * PL - 1
    pl.semaphore_wait(barrier, count)

    first = copies(
        [(1, 0, CN.at[1:4], ZC.at[0]), (-1, 0, CN.at[0:3], ZC.at[1]),
         (1, 0, DN.at[2:4], ZD.at[0]), (-1, 0, DN.at[0:2], ZD.at[1]),
         (0, 1, XS.at[0], XR.at[0]), (0, -1, XS.at[1], XR.at[1])]
        + [(dh, dj, GS.at[n], GR.at[n]) for n, (dh, dj) in enumerate(DIAGONALS)])
    start(first)

    def pair_rows(ref, first_row, rows):
        return ref[:, :, pl.ds(first_row, rows, stride=2), :] + ref[:, :, pl.ds(first_row + 1, rows, stride=2), :]

    S0[:, :, 4:20] = paired(c)
    own1 = 0.125 * pair_rows(S0, 4, 8)
    C1[4:6, :, 8:16] = own1
    S1[:, :, 8:16] = paired(own1)
    C2O[...] = 0.125 * pair_rows(S1, 8, 4)[0, 0]
    cond1 = tiles(C1, WIDE)
    start(cond1)
    gather_loop(lambda a, b: gather_copy(0, C2O, C2G, a, b).start())

    CA[3:7, :, 4:20] = c
    DA[2:6, :, 4:20] = d
    arrive(first)
    CA[0:3, :, 4:20] = ZC[0]
    CA[7:10, :, 4:20] = ZC[1]
    DA[0:2, :, 4:20] = ZD[0]
    DA[6:8, :, 4:20] = ZD[1]
    CA[3:7, :, 1:4] = XR[0, :, :, 0:3]
    CA[3:7, :, 20:23] = XR[1, :, :, 0:3]
    DA[2:6, :, 2:4] = XR[0, :, :, 3:5]
    DA[2:6, :, 20:22] = XR[1, :, :, 3:5]
    for n, (dh, dj) in enumerate(DIAGONALS):
        near, far, dnear = (2, 1, 1) if dh > 0 else (7, 8, 6)
        two, row = (2, 3) if dj > 0 else (20, 20)
        CA[near, :, two:two + 2] = GR[n, :, 0:2]
        CA[far, :, row:row + 1] = GR[n, :, 2:3]
        DA[dnear, :, row:row + 1] = GR[n, :, 3:4]

    def inside(z_count, z_first, z_total, rows, x_first, x_total):
        z = z_first + lax.broadcasted_iota(jnp.int32, (z_count, 1, rows, LANES), 0)
        x = x_first + lax.broadcasted_iota(jnp.int32, (z_count, 1, rows, LANES), 2)
        return (z >= 0) & (z < z_total) & (x >= 0) & (x < x_total)

    in0 = inside(10, 4 * h - 3, 4 * H, 24, 16 * j - 4, 16 * PL)
    k0 = setup(jnp.where(in0, CA[...], 1.0), in0[1:-1])
    f0 = jnp.where(in0[1:-1], DA[...], 0.0)
    p = k0[6] * f0
    k0 = trim(k0)
    f0 = f0[1:-1]
    p = sweep(p, f0, k0)
    PA[1:7] = p
    k0own = trim(k0)
    f0own = f0[1:-1]
    S0[...] = paired(residual(p, f0own, k0own))
    F1[4:6, :, 8:16] = 0.5 * pair_rows(S0, 4, 8)
    second = tiles(F1, AROUND)
    start(second)

    PN[...] = p[1:5, :, 4:20]
    for z in range(4):
        PXS[0, :, z:z + 1] = p[1 + z, :, 18:19]
        PXS[1, :, z:z + 1] = p[1 + z, :, 5:6]
    for n, (dh, dj) in enumerate(DIAGONALS):
        z = 4 if dh > 0 else 1
        row = 19 if dj > 0 else 4
        PGS[n, :, 0:1] = p[z, :, row:row + 1]
    spread = copies(
        [(1, 0, PN.at[2:3], PZ.at[0]), (-1, 0, PN.at[1:2], PZ.at[1]),
         (0, 1, PXS.at[0], PXR.at[0]), (0, -1, PXS.at[1], PXR.at[1])]
        + [(dh, dj, PGS.at[n], PGR.at[n]) for n, (dh, dj) in enumerate(DIAGONALS)])
    start(spread)

    arrive(cond1)
    in1 = inside(8, 2 * h - 3, 2 * H, 24, 8 * j - 8, 8 * PL)
    k1 = setup(jnp.where(in1, C1[1:9], 1.0), in1[1:-1])
    arrive(second)
    f1 = jnp.where(in1[1:-1], F1[2:8], 0.0)
    p1 = k1[6] * f1
    k1in = trim(k1)
    f1in = f1[1:-1]
    p1 = sweep(p1, f1in, k1in)
    P1[4:6, :, 8:16] = p1[1:3, :, 8:16]
    S1[...] = paired(residual(p1, f1in[1:-1], trim(k1in)))
    F2O[...] = 0.5 * pair_rows(S1, 8, 4)[0, 0]
    gather_loop(lambda a, b: gather_copy(1, F2O, F2G, a, b).start())
    third = tiles(P1, WIDE)
    start(third)

    def own_slot(ref):
        return ref.at[W if window else h, j]

    own_slot(C2G)[...] = C2O[...]
    own_slot(F2G)[...] = F2O[...]
    gather_in_loop(0, C2O, C2G)
    for b in range(PL):
        X2C[:, 4 * b:4 * b + 4, :] = C2G[:, b]
    zz = base + lax.broadcasted_iota(jnp.int32, (layers, 4 * PL, LANES), 0)
    in2 = (zz >= 0) & (zz < H)
    row = lax.broadcasted_iota(jnp.int32, (layers, 4 * PL, LANES), 1)

    def z_prev2(a, fill):
        return jnp.concatenate([jnp.full_like(a[:1], fill), a[:-1]], axis=0)

    def z_next2(a, fill):
        return jnp.concatenate([a[1:], jnp.full_like(a[:1], fill)], axis=0)

    def x_prev2(a, fill):
        return jnp.where(row == 0, fill, x_prev(a))

    def x_next2(a, fill):
        return jnp.where(row == 4 * PL - 1, fill, x_next(a))

    c2 = jnp.where(in2, X2C[...], 1.0)
    edge = harmonic(c2, jnp.ones_like(c2))
    zl = harmonic(c2, z_prev2(c2, 1.0))
    zu = jnp.concatenate([zl[1:], edge[-1:]], axis=0)
    xl = harmonic(c2, x_prev2(c2, 1.0))
    xu = jnp.where(row == 4 * PL - 1, edge, x_next(xl))
    yl = harmonic(c2, lane_prev(c2, 1.0))
    yu = lane_next(yl, edge)
    diag2 = zl + zu + xl + xu + yl + yu
    w2 = jnp.where(in2, OMEGA / diag2, 0.0)
    share = jnp.sum(diag2, axis=1, keepdims=True)

    def gathered2(q):
        return (zl * z_prev2(q, 0.0) + zu * z_next2(q, 0.0) + xl * x_prev2(q, 0.0) + xu * x_next2(q, 0.0)
                + yl * lane_prev(q, 0.0) + yu * lane_next(q, 0.0))

    gather_in_loop(1, F2O, F2G)
    for b in range(PL):
        X2F[:, 4 * b:4 * b + 4, :] = F2G[:, b]
    f2 = jnp.where(in2, X2F[...], 0.0)
    p2 = w2 * f2
    for _ in range(3):
        p2 = KEEP * p2 + w2 * (f2 + gathered2(p2))
    r2 = f2 - diag2 * p2 + gathered2(p2)
    line = jnp.sum(r2, axis=1, keepdims=True) / share
    p2 = jnp.where(in2, p2 + line, 0.0)
    blank = jnp.zeros((2, 4 * PL, LANES), F32)
    P2[0:2] = blank
    P2[2:2 + layers] = p2
    P2[2 + layers:4 + layers] = blank
    near2 = P2[pl.ds(W if window else h, 5)]
    side = jnp.zeros((5, 4, LANES), F32)
    wide2 = jnp.concatenate([side, near2, side], axis=1)
    mine2 = wide2[:, 0:12]
    for b in range(1, PL):
        mine2 = jnp.where(j == b, wide2[:, 4 * b:4 * b + 12], mine2)
    Q2[:, pl.ds(0, 12, stride=2), :] = mine2
    Q2[:, pl.ds(1, 12, stride=2), :] = mine2
    up2 = Q2[...]
    up2 = jnp.stack([up2[q] for q in (0, 1, 1, 2, 2, 3, 3, 4)], axis=0)[:, None]

    arrive(third)
    p1 = jnp.where(in1, P1[1:9] + up2, 0.0)
    p1 = sweep(p1, f1, k1)
    p1 = sweep(p1, f1in, k1in)
    Q1[:, :, pl.ds(0, 12, stride=2), :] = p1[:, :, 6:18]
    Q1[:, :, pl.ds(1, 12, stride=2), :] = p1[:, :, 6:18]
    up1 = Q1[...]

    arrive(spread)
    PA[0, :, 4:20] = PZ[0, 0]
    PA[7, :, 4:20] = PZ[1, 0]
    for z in range(4):
        PA[2 + z, :, 2:3] = PXR[0, :, z:z + 1]
        PA[2 + z, :, 21:22] = PXR[1, :, z:z + 1]
    for n, (dh, dj) in enumerate(DIAGONALS):
        z = 1 if dh > 0 else 6
        at = 3 if dj > 0 else 20
        PA[z, :, at:at + 1] = PGR[n, :, 0:1]
    fine = jnp.stack([jnp.stack([up1[z // 2, v // 2] for v in range(4)], axis=0) for z in range(8)], axis=0)
    p = jnp.where(in0[1:-1], PA[...] + fine, 0.0)
    p = sweep(p, f0, k0)
    p = sweep(p, f0own, k0own)
    p = p[:, :, 4:20]
    flat = jnp.concatenate([p[:, v].reshape(64, LANES) for v in range(4)], axis=1)
    back = lax.dot_general(split3(flat), order, (((1,), (1,)), ((), ())), preferred_element_type=F32)
    out_ref[...] = (back[0:64] + back[64:128] + back[128:192]).reshape(4, 16, 512)

    for made in (first, cond1, second, spread, third):
        sent(made)
    gather_loop(lambda a, b: gather_copy(0, C2O, C2G, a, b).wait_send())
    gather_loop(lambda a, b: gather_copy(1, F2O, F2G, a, b).wait_send())


def solution(mesh):
    H = mesh.shape["height"]
    PL = mesh.shape["plan"]
    window = H > 15
    W = 7
    layers = 2 * W + 1 if window else H
    copies = 10 + len(WIDE) + len(AROUND) + 8 + len(WIDE)

    def v(*shape):
        return pltpu.VMEM(shape + (LANES,), F32)

    scratch = [
        v(4, 4, 16), v(4, 4, 16),
        v(2, 3, 4, 16), v(2, 2, 4, 16),
        v(2, 4, 4, 8), v(2, 4, 4, 8),
        v(4, 4, 8), v(4, 4, 8),
        v(10, 4, 24), v(8, 4, 24),
        v(10, 2, 24), v(10, 2, 24), v(10, 2, 24),
        v(4), v(4), v(layers, PL, 4), v(layers, PL, 4),
        v(4, 4, 16), v(2, 1, 4, 16),
        v(2, 4, 8), v(2, 4, 8),
        v(4, 4, 8), v(4, 4, 8),
        v(8, 4, 24),
        v(2, 2, 24), v(1, 1, 24),
        v(5, 24), v(4, 2, 24),
        v(layers + 4, 4 * PL), v(layers, 4 * PL), v(layers, 4 * PL),
        pltpu.SemaphoreType.DMA((copies,)), pltpu.SemaphoreType.DMA((copies,)),
        pltpu.SemaphoreType.DMA((2, layers, PL)), pltpu.SemaphoreType.DMA((2, layers, PL)),
    ]

    def on_device(divergence, density, zones):
        return pl.pallas_call(
            functools.partial(kernel, H, PL, W, layers, window),
            out_shape=jax.ShapeDtypeStruct(divergence.shape, F32),
            in_specs=[pl.BlockSpec(memory_space=pltpu.VMEM)] * 3,
            out_specs=pl.BlockSpec(memory_space=pltpu.VMEM),
            scratch_shapes=scratch,
            compiler_params=pltpu.CompilerParams(
                collective_id=0, has_side_effects=True, vmem_limit_bytes=48 * 1024 * 1024),
            cost_estimate=pl.CostEstimate(flops=20_000_000, bytes_accessed=1_000_000, transcendentals=0),
            name="v_cycle",
        )(divergence, density, zones)

    spec = P("height", "plan", None)
    return jax.shard_map(on_device, mesh=mesh, in_specs=(spec, spec, spec), out_specs=spec, check_vma=False)
```

time: 256 us -> 31.8 us (0.12); the launches traced: 252 us -> 31.6 us
  starting transfers between devices: 120 us -> 0 us
  waiting for transfers between devices: 59.3 us -> 0 us
  local copies, waits for them, and re-layouts: 31.8 us -> 3.37 us
  Pallas kernels: 0 us -> 28.3 us
  blocking collectives: 25.1 us -> 0 us
  other arithmetic: 14.3 us -> 0 us
    ppermute x50 -> x0, starting transfers between devices: 120 us -> none  [the longest x25 87.7 us: padded_2(): lax.ppermute(tail, axis, [(i, (i + 1) % count) for i in range(ends)])]
    ppermute x50 -> x0, waiting for transfers between devices: 59.3 us -> none  [the longest x25 59 us: padded_2(): lax.ppermute(head, axis, [((i + 1) % count, i) for i in range(ends)])]
    pallas_call x0 -> x1, Pallas kernels: none -> 28.3 us  [on_device(): pl.pallas_call(functools.partial(kernel, H, PL, W, layers, window), out_s...]
    reshape x3 -> x0, local copies, waits for them, and re-layouts: 26.5 us -> none  [the longest x2 19.6 us: block_sum(): field.reshape(depth // 2, 2, across // 2, 2, along // 2, 2)]
    all_gather x2 -> x0, blocking collectives: 25.1 us -> none  [the longest x1 13.2 us: agglomerate(): lax.all_gather(cond, 'plan', axis=1, tiled=True)]
    reduce_sum x6 -> x0, other arithmetic: 8.52 us -> none  [the longest x5 8.42 us: block_sum(): field.reshape(depth // 2, 2, across // 2, 2, along // 2, 2)]
    broadcast_in_dim x3 -> x0, local copies, waits for them, and re-layouts: 4.25 us -> none  [prolong(): jnp.broadcast_to(field[:, None, :, None, :, None], (depth, 2, across, 2,...]
    unnamed x2 -> x7, local copies, waits for them, and re-layouts: 0.01 us -> 3.37 us
  transfers between devices with their start and end apart: 50 -> 0, of which waited for: 19 -> 0; matrix products, arithmetic and copies ran while one was open for 6% -> 0% of each run, Pallas kernels for 0% -> 0%
where the time goes in v1:
time: 31.8 us; the launch traced here: 31.6 us
  Pallas kernels  28.3 us (89%)
  local copies, waits for them, and re-layouts  3.37 us (11%)
    pallas_call x1, Pallas kernels, on_device(): pl.pallas_call(functools.partial(kernel, H, PL, W, layers, window), out_s...  28.3 us
    unnamed x7, local copies, waits for them, and re-layouts  3.37 us

profile of v1, /device:TPU:0, one launch (start us, length us, event | category | flops | bytes accessed | tf_op | source)
XLA Modules:
  0.0 31.6 jit_solution(1473081616690170022)
XLA Ops:
  0.0 0.0 copy-start
  0.0 0.9 %copy-done = f32[4,16,512]{2,1,0:T(8,128)S(1)} copy-done((f32[4,16,512]{2,1,0:T(8,128)S(1)}, f32[4,16,512]{2,1,0:T(8,128)}, u32[]{:S(2)}) %copy-start) | copy-done | bytes 131096
  0.9 0.0 copy-start.1
  0.9 0.9 %copy-done.1 = f32[4,16,512]{2,1,0:T(8,128)S(1)} copy-done((f32[4,16,512]{2,1,0:T(8,128)S(1)}, f32[4,16,512]{2,1,0:T(8,128)}, u32[]{:S(2)}) %copy-start.1) | copy-done | bytes 131096
  1.8 0.0 copy-start.2
  1.8 0.9 %copy-done.2 = s32[4,16,512]{2,1,0:T(8,128)S(1)} copy-done((s32[4,16,512]{2,1,0:T(8,128)S(1)}, s32[4,16,512]{2,1,0:T(8,128)}, u32[]{:S(2)}) %copy-start.2) | copy-done | bytes 131096
  2.7 28.3 %v_cycle.1 = f32[4,16,512]{2,1,0:T(8,128)S(1)} custom-call(f32[4,16,512]{2,1,0:T(8,128)S(1)} %copy-done, f32[4,16,512]{2,1,0:T(8,128)S(1)} %copy-done.1, s32[4,16,512]{2,1,0:T(8,128)S(1)} %copy-done.2), custom_call_target="tpu_custom_call" | custom-call | flops 20000000 | bytes 1000000 | tf_op jit(solution)/shard_map/v_cycle/pallas_call | solution.py:455
  31.0 0.7 %copy.5 = f32[4,16,512]{2,1,0:T(8,128)} copy(f32[4,16,512]{2,1,0:T(8,128)S(1)} %v_cycle.1) | data formatting | bytes 262144
Async XLA Ops:
  0.0 0.9 %copy-start = (f32[4,16,512]{2,1,0:T(8,128)S(1)}, f32[4,16,512]{2,1,0:T(8,128)}, u32[]{:S(2)}) copy-start(f32[4,16,512]{2,1,0:T(8,128)} %div_ref.1) | copy-start | bytes 393220
  0.9 0.9 %copy-start.1 = (f32[4,16,512]{2,1,0:T(8,128)S(1)}, f32[4,16,512]{2,1,0:T(8,128)}, u32[]{:S(2)}) copy-start(f32[4,16,512]{2,1,0:T(8,128)} %den_ref.1) | copy-start | bytes 393220
  1.8 0.9 %copy-start.2 = (s32[4,16,512]{2,1,0:T(8,128)S(1)}, s32[4,16,512]{2,1,0:T(8,128)}, u32[]{:S(2)}) copy-start(s32[4,16,512]{2,1,0:T(8,128)} %zon_ref.1) | copy-start | bytes 393220

commit v2 on v1

--- a/solution.py
+++ b/solution.py
@@ -20,8 +20,17 @@
 WIDE = tuple((a, b) for a in (-2, -1, 0, 1, 2) for b in (-1, 0, 1) if (a, b) != (0, 0))
 
 
+def inverse(a):
+    r = pl.reciprocal(a, approx=True)
+    return r * (2.0 - a * r)
+
+
 def harmonic(a, b):
-    return 2.0 * a * b / (a + b)
+    return (2.0 * a * b) * inverse(a + b)
+
+
+def wrap(a, count):
+    return jnp.where(a >= count, a - count, a)
 
 
 def lane_of(a):
@@ -60,7 +69,7 @@
     cyl = harmonic(m, y_prev(m, 1.0))
     cyu = y_next(cyl, harmonic(m[:, -1:], jnp.ones_like(m[:, -1:])))
     diag = cz[:-1] + cz[1:] + cx + cxl + cyl + cyu
-    w = jnp.where(inside, OMEGA / diag, 0.0)
+    w = jnp.where(inside, OMEGA * inverse(diag), 0.0)
     return (cz, cx, cxl, cyl, cyu, diag, w)
 
 
@@ -103,7 +112,11 @@
 def kernel(H, PL, W, layers, window, div_ref, den_ref, zon_ref, out_ref,
            CN, DN, ZC, ZD, XS, XR, GS, GR, CA, DA, C1, F1, P1, C2O, F2O, C2G, F2G,
            PN, PZ, PXS, PXR, PGS, PGR, PA, S0, S1, Q2, Q1, P2, X2C, X2F,
-           ssem, rsem, gssem, grsem):
+           DIN, ZIN, VIN, ssem, rsem, gssem, grsem, isem):
+    loads = [pltpu.make_async_copy(src, dst, isem.at[n])
+             for n, (src, dst) in enumerate(((zon_ref, ZIN), (den_ref, DIN), (div_ref, VIN)))]
+    for load in loads:
+        load.start()
     h = lax.axis_index("height")
     j = lax.axis_index("plan")
     base = h - W if window else 0
@@ -127,22 +140,24 @@
             def _():
                 for dj in range(PL):
                     if (dh, dj) != (0, 0):
-                        pl.semaphore_signal(barrier, inc=1, device_id=(h + dh, lax.rem(j + dj, PL)), device_id_type=MESH)
+                        pl.semaphore_signal(barrier, inc=1, device_id=(h + dh, wrap(j + dj, PL)), device_id_type=MESH)
     else:
         for a in range(H):
             for b in range(PL):
                 if (a, b) != (0, 0):
-                    pl.semaphore_signal(barrier, inc=1, device_id=(lax.rem(h + a, H), lax.rem(j + b, PL)), device_id_type=MESH)
-
-    zones = zon_ref[...]
+                    pl.semaphore_signal(barrier, inc=1, device_id=(wrap(h + a, H), wrap(j + b, PL)), device_id_type=MESH)
+
+    ys = lax.broadcasted_iota(jnp.int32, (512, 512), 0)
+    cs = lax.broadcasted_iota(jnp.int32, (512, 512), 1)
+    order = (ys == 4 * (cs % LANES) + cs // LANES).astype(F32).astype(jnp.bfloat16)
+    for load in loads:
+        load.wait()
+    zones = ZIN[...]
     perm = jnp.zeros(zones.shape, F32)
     for zone_id, value in enumerate(PERMEABILITY):
         perm = jnp.where(zones == zone_id, F32(value), perm)
-    cond = perm / den_ref[...]
-    ys = lax.broadcasted_iota(jnp.int32, (512, 512), 0)
-    cs = lax.broadcasted_iota(jnp.int32, (512, 512), 1)
-    order = (ys == 4 * (cs % LANES) + cs // LANES).astype(F32).astype(jnp.bfloat16)
-    both = jnp.concatenate([cond.reshape(64, 512), div_ref[...].reshape(64, 512)], axis=0)
+    cond = perm * inverse(DIN[...])
+    both = jnp.concatenate([cond.reshape(64, 512), VIN[...].reshape(64, 512)], axis=0)
     moved = jnp.dot(split3(both), order, preferred_element_type=F32)
     moved = moved[0:128] + moved[128:256] + moved[256:384]
     for v in range(4):
@@ -188,9 +203,14 @@
         for there, _, copy in made:
             pl.when(there)(copy.wait_send)
 
-    def tiles(ref, around):
-        return copies([(dh, dj, ref.at[4:6, :, 8:16], ref.at[4 - 2 * dh:6 - 2 * dh, :, 8 - 8 * dj:16 - 8 * dj])
-                       for dh, dj in around])
+    def tiles(ref, around, rows):
+        items = []
+        for dh, dj in around:
+            z0, z1 = {2: (5, 6), -2: (4, 5)}.get(dh, (4, 6))
+            x0, x1 = {1: (16 - rows, 16), -1: (8, 8 + rows)}.get(dj, (8, 16))
+            items.append((dh, dj, ref.at[z0:z1, :, x0:x1],
+                          ref.at[z0 - 2 * dh:z1 - 2 * dh, :, x0 - 8 * dj:x1 - 8 * dj]))
+        return copies(items)
 
     def gather_loop(act):
         if window:
@@ -209,10 +229,10 @@
         if window:
             to, mine, n = h + a, W - a, a + W
         else:
-            to, mine, n = lax.rem(h + a, H), h, a
+            to, mine, n = wrap(h + a, H), h, a
         return pltpu.make_async_remote_copy(
             src_ref=src, dst_ref=buf.at[mine, j], send_sem=gssem.at[which, n, b],
-            recv_sem=grsem.at[which, n, b], device_id=(to, lax.rem(j + b, PL)), device_id_type=MESH)
+            recv_sem=grsem.at[which, n, b], device_id=(to, wrap(j + b, PL)), device_id_type=MESH)
 
     def gather_in(which, src, buf, a, b):
         gather_copy(which, src, buf, a, b).wait_recv()
@@ -239,8 +259,8 @@
     first = copies(
         [(1, 0, CN.at[1:4], ZC.at[0]), (-1, 0, CN.at[0:3], ZC.at[1]),
          (1, 0, DN.at[2:4], ZD.at[0]), (-1, 0, DN.at[0:2], ZD.at[1]),
-         (0, 1, XS.at[0], XR.at[0]), (0, -1, XS.at[1], XR.at[1])]
-        + [(dh, dj, GS.at[n], GR.at[n]) for n, (dh, dj) in enumerate(DIAGONALS)])
+         (0, 1, XS.at[0, :, :, 0:5], XR.at[0, :, :, 0:5]), (0, -1, XS.at[1, :, :, 0:5], XR.at[1, :, :, 0:5])]
+        + [(dh, dj, GS.at[n, :, 0:4], GR.at[n, :, 0:4]) for n, (dh, dj) in enumerate(DIAGONALS)])
     start(first)
 
     def pair_rows(ref, first_row, rows):
@@ -251,7 +271,7 @@
     C1[4:6, :, 8:16] = own1
     S1[:, :, 8:16] = paired(own1)
     C2O[...] = 0.125 * pair_rows(S1, 8, 4)[0, 0]
-    cond1 = tiles(C1, WIDE)
+    cond1 = tiles(C1, WIDE, 3)
     start(cond1)
     gather_loop(lambda a, b: gather_copy(0, C2O, C2G, a, b).start())
 
@@ -290,7 +310,7 @@
     f0own = f0[1:-1]
     S0[...] = paired(residual(p, f0own, k0own))
     F1[4:6, :, 8:16] = 0.5 * pair_rows(S0, 4, 8)
-    second = tiles(F1, AROUND)
+    second = tiles(F1, AROUND, 2)
     start(second)
 
     PN[...] = p[1:5, :, 4:20]
@@ -303,8 +323,8 @@
         PGS[n, :, 0:1] = p[z, :, row:row + 1]
     spread = copies(
         [(1, 0, PN.at[2:3], PZ.at[0]), (-1, 0, PN.at[1:2], PZ.at[1]),
-         (0, 1, PXS.at[0], PXR.at[0]), (0, -1, PXS.at[1], PXR.at[1])]
-        + [(dh, dj, PGS.at[n], PGR.at[n]) for n, (dh, dj) in enumerate(DIAGONALS)])
+         (0, 1, PXS.at[0, :, 0:4], PXR.at[0, :, 0:4]), (0, -1, PXS.at[1, :, 0:4], PXR.at[1, :, 0:4])]
+        + [(dh, dj, PGS.at[n, :, 0:1], PGR.at[n, :, 0:1]) for n, (dh, dj) in enumerate(DIAGONALS)])
     start(spread)
 
     arrive(cond1)
@@ -320,7 +340,7 @@
     S1[...] = paired(residual(p1, f1in[1:-1], trim(k1in)))
     F2O[...] = 0.5 * pair_rows(S1, 8, 4)[0, 0]
     gather_loop(lambda a, b: gather_copy(1, F2O, F2G, a, b).start())
-    third = tiles(P1, WIDE)
+    third = tiles(P1, WIDE, 3)
     start(third)
 
     def own_slot(ref):
@@ -356,7 +376,7 @@
     yl = harmonic(c2, lane_prev(c2, 1.0))
     yu = lane_next(yl, edge)
     diag2 = zl + zu + xl + xu + yl + yu
-    w2 = jnp.where(in2, OMEGA / diag2, 0.0)
+    w2 = jnp.where(in2, OMEGA * inverse(diag2), 0.0)
     share = jnp.sum(diag2, axis=1, keepdims=True)
 
     def gathered2(q):
@@ -447,15 +467,17 @@
         v(2, 2, 24), v(1, 1, 24),
         v(5, 24), v(4, 2, 24),
         v(layers + 4, 4 * PL), v(layers, 4 * PL), v(layers, 4 * PL),
+        pltpu.VMEM((4, 16, 512), F32), pltpu.VMEM((4, 16, 512), jnp.int32), pltpu.VMEM((4, 16, 512), F32),
         pltpu.SemaphoreType.DMA((copies,)), pltpu.SemaphoreType.DMA((copies,)),
         pltpu.SemaphoreType.DMA((2, layers, PL)), pltpu.SemaphoreType.DMA((2, layers, PL)),
+        pltpu.SemaphoreType.DMA((3,)),
     ]
 
     def on_device(divergence, density, zones):
         return pl.pallas_call(
             functools.partial(kernel, H, PL, W, layers, window),
             out_shape=jax.ShapeDtypeStruct(divergence.shape, F32),
-            in_specs=[pl.BlockSpec(memory_space=pltpu.VMEM)] * 3,
+            in_specs=[pl.BlockSpec(memory_space=pltpu.HBM)] * 3,
             out_specs=pl.BlockSpec(memory_space=pltpu.VMEM),
             scratch_shapes=scratch,
             compiler_params=pltpu.CompilerParams(

time: 31.8 us -> 29.8 us (0.937)
  Pallas kernels: 28.3 us -> 26.3 us
    pallas_call x1, Pallas kernels: 28.3 us -> 26.3 us  [on_device(): pl.pallas_call(functools.partial(kernel, H, PL, W, layers, window), out_s...]
where the time goes in v2:
time: 29.8 us; the launch traced here: 29.7 us
  Pallas kernels  26.3 us (88%)
  local copies, waits for them, and re-layouts  3.37 us (11%)
    pallas_call x1, Pallas kernels, on_device(): pl.pallas_call(functools.partial(kernel, H, PL, W, layers, window), out_s...  26.3 us
    unnamed x7, local copies, waits for them, and re-layouts  3.37 us

profile of v2, /device:TPU:0, one launch (start us, length us, event | category | flops | bytes accessed | tf_op | source)
XLA Modules:
  0.0 29.7 jit_solution(3765777069859326830)
XLA Ops:
  0.0 0.0 copy-start
  0.0 0.9 %copy-done = f32[4,16,512]{2,1,0:T(8,128)S(1)} copy-done((f32[4,16,512]{2,1,0:T(8,128)S(1)}, f32[4,16,512]{2,1,0:T(8,128)}, u32[]{:S(2)}) %copy-start) | copy-done | bytes 131096
  0.9 0.0 copy-start.1
  0.9 0.9 %copy-done.1 = f32[4,16,512]{2,1,0:T(8,128)S(1)} copy-done((f32[4,16,512]{2,1,0:T(8,128)S(1)}, f32[4,16,512]{2,1,0:T(8,128)}, u32[]{:S(2)}) %copy-start.1) | copy-done | bytes 131096
  1.8 0.0 copy-start.2
  1.8 0.9 %copy-done.2 = s32[4,16,512]{2,1,0:T(8,128)S(1)} copy-done((s32[4,16,512]{2,1,0:T(8,128)S(1)}, s32[4,16,512]{2,1,0:T(8,128)}, u32[]{:S(2)}) %copy-start.2) | copy-done | bytes 131096
  2.7 26.3 %v_cycle.1 = f32[4,16,512]{2,1,0:T(8,128)S(1)} custom-call(f32[4,16,512]{2,1,0:T(8,128)S(1)} %copy-done, f32[4,16,512]{2,1,0:T(8,128)S(1)} %copy-done.1, s32[4,16,512]{2,1,0:T(8,128)S(1)} %copy-done.2), custom_call_target="tpu_custom_call" | custom-call | flops 20000000 | bytes 1000000 | tf_op jit(solution)/shard_map/v_cycle/pallas_call | solution.py:477
  29.0 0.7 %copy.5 = f32[4,16,512]{2,1,0:T(8,128)} copy(f32[4,16,512]{2,1,0:T(8,128)S(1)} %v_cycle.1) | data formatting | bytes 262144
Async XLA Ops:
  0.0 0.9 %copy-start = (f32[4,16,512]{2,1,0:T(8,128)S(1)}, f32[4,16,512]{2,1,0:T(8,128)}, u32[]{:S(2)}) copy-start(f32[4,16,512]{2,1,0:T(8,128)} %div_ref.1) | copy-start | bytes 393220
  0.9 0.9 %copy-start.1 = (f32[4,16,512]{2,1,0:T(8,128)S(1)}, f32[4,16,512]{2,1,0:T(8,128)}, u32[]{:S(2)}) copy-start(f32[4,16,512]{2,1,0:T(8,128)} %den_ref.1) | copy-start | bytes 393220
  1.8 0.9 %copy-start.2 = (s32[4,16,512]{2,1,0:T(8,128)S(1)}, s32[4,16,512]{2,1,0:T(8,128)}, u32[]{:S(2)}) copy-start(s32[4,16,512]{2,1,0:T(8,128)} %zon_ref.1) | copy-start | bytes 393220

commit v3 on v2

--- a/solution.py
+++ b/solution.py
@@ -273,7 +273,6 @@
     C2O[...] = 0.125 * pair_rows(S1, 8, 4)[0, 0]
     cond1 = tiles(C1, WIDE, 3)
     start(cond1)
-    gather_loop(lambda a, b: gather_copy(0, C2O, C2G, a, b).start())
 
     CA[3:7, :, 4:20] = c
     DA[2:6, :, 4:20] = d
@@ -326,6 +325,8 @@
          (0, 1, PXS.at[0, :, 0:4], PXR.at[0, :, 0:4]), (0, -1, PXS.at[1, :, 0:4], PXR.at[1, :, 0:4])]
         + [(dh, dj, PGS.at[n, :, 0:1], PGR.at[n, :, 0:1]) for n, (dh, dj) in enumerate(DIAGONALS)])
     start(spread)
+
+    gather_loop(lambda a, b: gather_copy(0, C2O, C2G, a, b).start())
 
     arrive(cond1)
     in1 = inside(8, 2 * h - 3, 2 * H, 24, 8 * j - 8, 8 * PL)
@@ -481,7 +482,7 @@
             out_specs=pl.BlockSpec(memory_space=pltpu.VMEM),
             scratch_shapes=scratch,
             compiler_params=pltpu.CompilerParams(
-                collective_id=0, has_side_effects=True, vmem_limit_bytes=48 * 1024 * 1024),
+                collective_id=0, has_side_effects=True),
             cost_estimate=pl.CostEstimate(flops=20_000_000, bytes_accessed=1_000_000, transcendentals=0),
             name="v_cycle",
         )(divergence, density, zones)

time: 29.8 us -> 27.3 us (0.916)
  local copies, waits for them, and re-layouts: 3.37 us -> 1.57 us
  Pallas kernels: 26.3 us -> 25.6 us
    unnamed x7 -> x1, local copies, waits for them, and re-layouts: 3.37 us -> 1.57 us
    pallas_call x1, Pallas kernels: 26.3 us -> 25.6 us  [on_device(): pl.pallas_call(functools.partial(kernel, H, PL, W, layers, window), out_s...]
where the time goes in v3:
time: 27.3 us; the launch traced here: 27.2 us
  Pallas kernels  25.6 us (94%)
  local copies, waits for them, and re-layouts  1.57 us (6%)
    pallas_call x1, Pallas kernels, on_device(): pl.pallas_call(functools.partial(kernel, H, PL, W, layers, window), out_s...  25.6 us
    unnamed x1, local copies, waits for them, and re-layouts  1.57 us

profile of v3, /device:TPU:0, one launch (start us, length us, event | category | flops | bytes accessed | tf_op | source)
XLA Modules:
  0.0 27.2 jit_solution(6183419879488091042)
XLA Ops:
  0.0 25.6 %v_cycle.1 = f32[4,16,512]{2,1,0:T(8,128)} custom-call(f32[4,16,512]{2,1,0:T(8,128)} %div_ref.1, f32[4,16,512]{2,1,0:T(8,128)} %den_ref.1, s32[4,16,512]{2,1,0:T(8,128)} %zon_ref.1), custom_call_target="tpu_custom_call" | custom-call | flops 20000000 | bytes 1000000 | tf_op jit(solution)/shard_map/v_cycle/pallas_call | solution.py:478
  25.6 1.6 %copy.5 = f32[4,16,512]{2,1,0:T(8,128)} copy(f32[4,16,512]{2,1,0:T(8,128)} %v_cycle.1) | data formatting | bytes 262144

commit v4 on v3

--- a/solution.py
+++ b/solution.py
@@ -384,6 +384,9 @@
         return (zl * z_prev2(q, 0.0) + zu * z_next2(q, 0.0) + xl * x_prev2(q, 0.0) + xu * x_next2(q, 0.0)
                 + yl * lane_prev(q, 0.0) + yu * lane_next(q, 0.0))
 
+    for made in (first, cond1, second, spread):
+        sent(made)
+    gather_loop(lambda a, b: gather_copy(0, C2O, C2G, a, b).wait_send())
     gather_in_loop(1, F2O, F2G)
     for b in range(PL):
         X2F[:, 4 * b:4 * b + 4, :] = F2G[:, b]
@@ -436,9 +439,7 @@
     back = lax.dot_general(split3(flat), order, (((1,), (1,)), ((), ())), preferred_element_type=F32)
     out_ref[...] = (back[0:64] + back[64:128] + back[128:192]).reshape(4, 16, 512)
 
-    for made in (first, cond1, second, spread, third):
-        sent(made)
-    gather_loop(lambda a, b: gather_copy(0, C2O, C2G, a, b).wait_send())
+    sent(third)
     gather_loop(lambda a, b: gather_copy(1, F2O, F2G, a, b).wait_send())
 
 

time: 27.3 us -> 27.2 us (level)
  no operation moved by 1% of the time
where the time goes in v4:
time: 27.2 us; the launch traced here: 27.1 us
  Pallas kernels  25.5 us (94%)
  local copies, waits for them, and re-layouts  1.57 us (6%)
    pallas_call x1, Pallas kernels, on_device(): pl.pallas_call(functools.partial(kernel, H, PL, W, layers, window), out_s...  25.5 us
    unnamed x1, local copies, waits for them, and re-layouts  1.57 us

profile of v4, /device:TPU:0, one launch (start us, length us, event | category | flops | bytes accessed | tf_op | source)
XLA Modules:
  0.0 27.1 jit_solution(8058383867234937292)
XLA Ops:
  0.0 25.5 %v_cycle.1 = f32[4,16,512]{2,1,0:T(8,128)} custom-call(f32[4,16,512]{2,1,0:T(8,128)} %div_ref.1, f32[4,16,512]{2,1,0:T(8,128)} %den_ref.1, s32[4,16,512]{2,1,0:T(8,128)} %zon_ref.1), custom_call_target="tpu_custom_call" | custom-call | flops 20000000 | bytes 1000000 | tf_op jit(solution)/shard_map/v_cycle/pallas_call | solution.py:479
  25.5 1.6 %copy.5 = f32[4,16,512]{2,1,0:T(8,128)} copy(f32[4,16,512]{2,1,0:T(8,128)} %v_cycle.1) | data formatting | bytes 262144
